TPU v7x, 512 devices: a whole 4x4x16 slice. The times are simulated.
512 devices in a mesh: sub: 64 (over z_lo, y, core), strip: 8 (over x, z_hi).
Axes of the slice: x: 4, y: 4, z: 16 (z_hi: 2, z_lo: 8; z = z_hi * 8 + z_lo), core: 2. Of those that a mesh axis runs over, the one named last changes fastest.
Arguments:
- spectra: bfloat16 [128, 256, 2048], P('sub', 'strip'), may hold values from -6 to 6
- offsets: int32 [128], P('sub'), may hold values from 0 to 1023
Outputs:
- foreground: float32 [1024, 256, 128], P('strip', 'sub')
All inputs are finite; a program needn't handle non-finite values.
Results may differ from a plain program's by a relative error of at most 0.0068.
Values may be sent and summed in bfloat16 or wider, within the bound.
No kernel may reach another device: no remote copies, remote signals or barrier semaphores. Data moves between devices by JAX's collectives and lax.ppermute only.
A program may use at most 64 MiB of HBM per device.

v0:
```python
import math
import jax
import jax.numpy as jnp
import numpy as np
from jax import lax
from jax.sharding import PartitionSpec as P

KR = 256
ROWS = 1024
COLS = 256
WIN = 8
BG = 16


def from_behind(value, axis, steps):
    count = lax.axis_size(axis)
    pairs = [(source, (source + steps) % count) for source in range(count)]
    return lax.ppermute(value, axis, pairs)


def extended(shard, sides, width):
    for axis, dim in sides:
        count, length = (lax.axis_size(axis), shard.shape[dim])
        up = [(i, (i + 1) % count) for i in range(count - 1)]
        down = [(j, i) for i, j in up]
        last = lax.slice_in_dim(shard, length - width, length, axis=dim)
        leading = lax.slice_in_dim(shard, 0, width, axis=dim)
        before = lax.ppermute(last, axis, up)
        after = lax.ppermute(leading, axis, down)
        shard = jnp.concatenate([before, shard, after], axis=dim)
    return shard


def column_table(samples, width):
    sample_index = jnp.arange(samples, dtype=jnp.int32)[:, None]
    column_index = jnp.arange(width, dtype=jnp.int32)[None, :]
    phase = jnp.mod(sample_index * column_index, samples).astype(jnp.float32) * (
        2.0 * math.pi / samples
    )
    cosine = jnp.cos(phase) / math.sqrt(samples)
    sine = -jnp.sin(phase) / math.sqrt(samples)
    upper = jnp.concatenate([cosine, sine], axis=1)
    lower = jnp.concatenate([-sine, cosine], axis=1)
    return jnp.concatenate([upper, lower], axis=0).astype(jnp.bfloat16)


def row_table(row_index, samples, image_rows):
    sample_index = jnp.arange(samples, dtype=jnp.int32)[None, :] - samples // 2
    phase = jnp.mod(row_index[:, None] * sample_index, image_rows).astype(jnp.float32) * (
        2.0 * math.pi / image_rows
    )
    scale = 1.0 / math.sqrt(samples)
    return jnp.concatenate([jnp.cos(phase) * scale, jnp.sin(phase) * scale], axis=0).astype(
        jnp.bfloat16
    )


def apply_phase(mixed, offsets, sample_index):
    angle = jnp.mod(offsets[:, None] * (sample_index[None, :] - KR // 2), ROWS).astype(
        jnp.float32
    ) * (2.0 * math.pi / ROWS)
    cosine = jnp.cos(angle)[:, :, None]
    sine = jnp.sin(angle)[:, :, None]
    real_part = mixed[:, :, :COLS]
    imag_part = mixed[:, :, COLS:]
    return jnp.concatenate(
        [real_part * cosine - imag_part * sine, real_part * sine + imag_part * cosine], axis=2
    ).astype(jnp.bfloat16)


def window_mask(block_offset, count):
    target = np.arange(count)[:, None]
    source = np.arange(count)[None, :]
    distance = block_offset * count + source - target
    return ((distance >= 0) & (distance < WIN)).astype(np.float32)


def combine_parts(product, strip_rows):
    product = lax.optimization_barrier(product)
    real_part = product[:, :strip_rows, :COLS] - product[:, strip_rows:, COLS:]
    imag_part = product[:, :strip_rows, COLS:] + product[:, strip_rows:, :COLS]
    return jnp.concatenate([real_part, imag_part], axis=2)


def remove_background(stack):
    frame_count = stack.shape[0]
    series = jnp.transpose(stack, (1, 2, 0))
    source = jnp.arange(frame_count, dtype=jnp.int32)[:, None]
    target = jnp.arange(frame_count, dtype=jnp.int32)[None, :]
    behind = jnp.where(jnp.mod(target - source, frame_count) < BG, 1.0 / BG, 0.0).astype(
        jnp.float32
    )
    weights = jnp.where(source == target, 1.0, 0.0).astype(jnp.float32) - behind
    return jnp.einsum("rcg,gf->rcf", series, weights, precision=lax.Precision.HIGHEST)


def body(spectra, offsets):
    sub_dev = spectra.shape[0]
    strip_rows = ROWS // lax.axis_size("strip")
    first_row = lax.axis_index("strip") * strip_rows
    own_rows = first_row + jnp.arange(strip_rows, dtype=jnp.int32)
    columns = column_table(spectra.shape[2] // 2, COLS)
    table = row_table(own_rows, KR, ROWS)
    passes = (WIN - 2 + sub_dev) // sub_dev
    piece = lax.all_gather(spectra, "strip", axis=1, tiled=True)
    sample_index = jnp.arange(piece.shape[1], dtype=jnp.int32)
    shifted = apply_phase(
        jnp.einsum("skc,cn->skn", piece, columns, preferred_element_type=jnp.float32),
        offsets,
        sample_index,
    )
    product = jnp.einsum("mk,skn->smn", table, shifted, preferred_element_type=jnp.float32)
    images = combine_parts(product, strip_rows)
    frames = jnp.einsum(
        "ab,bmn->amn", jnp.asarray(window_mask(0, sub_dev)), images, precision=lax.Precision.HIGHEST
    )
    moving = images
    for block_offset in range(1, passes + 1):
        moving = from_behind(moving, "sub", -1)
        frames = frames + jnp.einsum(
            "ab,bmn->amn",
            jnp.asarray(window_mask(block_offset, sub_dev)),
            moving,
            precision=lax.Precision.HIGHEST,
        )
    real_part = frames[:, :, :COLS]
    imag_part = frames[:, :, COLS:]
    log_power = jnp.log(1.0 + real_part * real_part + imag_part * imag_part)
    padded = extended(log_power, (("strip", 1),), 1)
    padded = jnp.pad(padded, ((0, 0), (0, 0), (1, 1)))
    total = jnp.zeros_like(log_power)
    for row_step in range(3):
        for col_step in range(3):
            total = total + padded[:, row_step : row_step + strip_rows, col_step : col_step + COLS]
    filtered = total / 9.0
    return remove_background(
        lax.all_to_all(filtered, "sub", split_axis=2, concat_axis=0, tiled=True)
    )


def solution(mesh):
    in_specs = (P("sub", "strip", None), P("sub"))
    out_specs = P("strip", "sub", None)
    return jax.shard_map(body, mesh=mesh, in_specs=in_specs, out_specs=out_specs, check_vma=False)
```

profile of v0, /device:TPU:1, one launch (start us, length us, event | category | flops | bytes accessed | tf_op | source)
XLA Modules:
  0.0 272.1 jit_solution(287190779689159328)
XLA Ops:
  6.5 0.0 all-gather.2.cloned.1.call-start
  6.5 0.7 all-gather.2.cloned.1.call-update
  7.3 4.0 %fusion.15 = bf16[1024,256]{0,1:T(8,128)(2,1)S(1)} fusion(), kind=kLoop, calls=%fused_computation.27 | loop fusion | flops 4456448 | bytes 524288 | tf_op jit(solution)/shard_map/convert.9
  11.2 4.3 %negate_convert_fusion = (bf16[1024,256]{0,1:T(8,128)(2,1)S(1)}, bf16[1024,256]{0,1:T(8,128)(2,1)S(1)}) fusion(), kind=kLoop, calls=%fused_computation.21 | loop fusion | flops 5242880 | bytes 1048576 | tf_op jit(solution)/shard_map/convert.6
  15.6 0.8 fusion.55
  16.4 0.6 multiply_convert_fusion.2
  17.0 115.6 %all-gather.2.cloned.1.call-done = bf16[2,256,2048]{2,1,0:T(8,128)(2,1)} async-done(((bf16[2,32,2048]{2,1,0:T(8,128)(2,1)}), bf16[2,256,2048]{2,1,0:T(8,128)(2,1)}) %all-gather.2.cloned.1.call-update) | async-done | bytes 2097168 | tf_op jit(solution)/shard_map/all_gather | solution.py:105
  132.6 2.9 %fusion.7 = f32[2,256,512]{1,2,0:T(8,128)S(1)} fusion(bf16[2,256,2048]{2,1,0:T(8,128)(2,1)} %all-gather.2.cloned.1.call-done, bf16[1024,256]{0,1:T(8,128)(2,1)S(1)} %get-tuple-element.16, bf16[1024,256]{0,1:T(8,128)(2,1)S(1)} %get-tuple-element.15, bf16[1024,256]{0,1:T(8,128)(2,1)S(1)} %fusion.15), kind=kOutput, calls=%fused_computation.11 | convolution fusion | flops 1082130432 | bytes 4718592 | tf_op jit(solution)/shard_map/skc,cn->skn/dot_general | solution.py:108
  135.5 0.1 subtract_convert_fusion
  135.6 0.3 convolution_bitcast_fusion
  136.0 0.0 copy-start
  136.0 0.1 slice_subtract_fusion
  136.1 4.1 %collective-permute-start = (f32[2,128,512]{1,2,0:T(8,128)S(1)}, f32[2,128,512]{1,2,0:T(8,128)S(1)}, u32[]{:S(2)}, u32[]{:S(2)}) collective-permute-start(f32[2,128,512]{1,2,0:T(8,128)S(1)} %pad_maximum_fusion), channel_id=1, source_target_pairs={{0,504},{8,0},{16,8},{24,16},{32,24},{40,32},{48,40},{56,48},{64,5... | collective-permute-start | bytes 1572872 | tf_op jit(solution)/shard_map/ppermute | solution.py:18
  140.2 6.4 %collective-permute-done = f32[2,128,512]{1,2,0:T(8,128)S(1)} collective-permute-done((f32[2,128,512]{1,2,0:T(8,128)S(1)}, f32[2,128,512]{1,2,0:T(8,128)S(1)}, u32[]{:S(2)}, u32[]{:S(2)}) %collective-permute-start) | collective-permute-done | bytes 524320 | tf_op jit(solution)/shard_map/ppermute | solution.py:18
  146.6 3.4 %collective-permute-start.1 = (f32[2,128,512]{1,2,0:T(8,128)S(1)}, f32[2,128,512]{1,2,0:T(8,128)S(1)}, u32[]{:S(2)}, u32[]{:S(2)}) collective-permute-start(f32[2,128,512]{1,2,0:T(8,128)S(1)} %collective-permute-done), channel_id=1, source_target_pairs={{0,504},{8,0},{16,8},{24,16},{32,24},{40,32},{48,40},{56,48},{64,5... | collective-permute-start | bytes 1572872 | tf_op jit(solution)/shard_map/ppermute | solution.py:18
  150.0 7.1 %collective-permute-done.1 = f32[2,128,512]{1,2,0:T(8,128)S(1)} collective-permute-done((f32[2,128,512]{1,2,0:T(8,128)S(1)}, f32[2,128,512]{1,2,0:T(8,128)S(1)}, u32[]{:S(2)}, u32[]{:S(2)}) %collective-permute-start.1) | collective-permute-done | bytes 524320 | tf_op jit(solution)/shard_map/ppermute | solution.py:18
  157.1 12.1 %collective-permute-start.2 = (f32[2,128,512]{1,2,0:T(8,128)S(1)}, f32[2,128,512]{1,2,0:T(8,128)S(1)}, u32[]{:S(2)}, u32[]{:S(2)}) collective-permute-start(f32[2,128,512]{1,2,0:T(8,128)S(1)} %collective-permute-done.1), channel_id=1, source_target_pairs={{0,504},{8,0},{16,8},{24,16},{32,24},{40,32},{48,40},{56,48},{64,5... | collective-permute-start | bytes 1572872 | tf_op jit(solution)/shard_map/ppermute | solution.py:18
  169.2 0.2 copy.34
  169.4 0.0 copy-done
  169.4 1.9 fusion.72
  171.3 0.2 copy.35
  171.6 2.0 convolution_add_fusion.3
  173.6 0.2 copy.36
  173.8 0.0 collective-permute-done.2
  173.9 14.7 %collective-permute-start.3 = (f32[2,128,512]{1,2,0:T(8,128)S(1)}, f32[2,128,512]{1,2,0:T(8,128)S(1)}, u32[]{:S(2)}, u32[]{:S(2)}) collective-permute-start(f32[2,128,512]{1,2,0:T(8,128)S(1)} %collective-permute-done.2), channel_id=1, source_target_pairs={{0,504},{8,0},{16,8},{24,16},{32,24},{40,32},{48,40},{56,48},{64,5... | collective-permute-start | bytes 1572872 | tf_op jit(solution)/shard_map/ppermute | solution.py:18
  188.6 2.0 convolution_add_fusion.2
  190.6 0.0 copy-start.1
  190.6 0.2 copy.37
  190.8 2.0 convolution_add_fusion.1
  192.9 0.0 collective-permute-done.3
  192.9 0.2 copy.38
  193.1 0.0 copy-done.1
  193.1 2.0 fusion.8
  195.2 0.2 fusion.24
  195.4 8.6 %collective-permute-start.4 = (f32[2,1,256]{2,0,1:T(2,128)S(1)}, f32[2,1,256]{2,0,1:T(2,128)S(1)}, u32[]{:S(2)}, u32[]{:S(2)}) collective-permute-start(f32[2,1,256]{2,0,1:T(2,128)S(1)} %get-tuple-element.9), channel_id=1, source_target_pairs={{0,1},{1,2},{2,3},{3,4},{4,5},{5,6},{6,7},{8,9},{9,10},{10,11},{11... | collective-permute-start | bytes 6152 | tf_op jit(solution)/shard_map/ppermute | solution.py:28
  204.0 1.3 collective-permute-start.5
  205.3 0.0 collective-permute-done.4
  205.3 11.7 %collective-permute-done.5 = f32[2,1,256]{2,0,1:T(2,128)S(1)} collective-permute-done((f32[2,1,256]{2,0,1:T(2,128)S(1)}, f32[2,1,256]{2,0,1:T(2,128)S(1)}, u32[]{:S(2)}, u32[]{:S(2)}) %collective-permute-start.5) | collective-permute-done | bytes 2080 | tf_op jit(solution)/shard_map/ppermute | solution.py:29
  217.0 0.5 select_maximum_fusion
  217.5 1.0 fusion.19
  218.4 0.2 copy.39
  218.6 45.0 %all_to_all.18 = f32[2,128,256]{1,0,2:T(2,128)S(1)} all-to-all(f32[2,128,256]{1,0,2:T(2,128)S(1)} %copy.39), channel_id=1, replica_groups=mesh['sub'=64,'strip'=8] {'sub'}, dimensions={2} | all-to-all | bytes 524288 | tf_op jit(solution)/shard_map/all_to_all | solution.py:137
  263.6 0.2 copy.41
  263.9 0.1 copy.42
  264.0 0.4 fusion.26
  264.4 0.9 copy.43
  (5 shorter events, 0.1 us)
Async XLA Ops:
  6.5 126.1 %all-gather.2.cloned.1.call-start = ((), (), s32[]{:S(2)}) async-start(), calls=%async_computation.1 | async-start | bytes 2359296 | tf_op jit(solution)/shard_map/all_gather | solution.py:105
  136.0 33.5 %copy-start = (f32[2,2,1]{1,0,2:T(2,128)S(1)}, f32[2,2,1]{1,0,2:T(2,128)}, u32[]{:S(2)}) copy-start(f32[2,2,1]{1,0,2:T(2,128)} %constant.88) | copy-start | bytes 52
  136.1 10.5 %collective-permute-start = (f32[2,128,512]{1,2,0:T(8,128)S(1)}, f32[2,128,512]{1,2,0:T(8,128)S(1)}, u32[]{:S(2)}, u32[]{:S(2)}) collective-permute-start(f32[2,128,512]{1,2,0:T(8,128)S(1)} %pad_maximum_fusion), channel_id=1, source_target_pairs={{0,504},{8,0},{16,8},{24,16},{32,24},{40,32},{48,40},{56,48},{64,5... | collective-permute-start | bytes 1572872 | tf_op jit(solution)/shard_map/ppermute | solution.py:18
  146.6 10.5 %collective-permute-start.1 = (f32[2,128,512]{1,2,0:T(8,128)S(1)}, f32[2,128,512]{1,2,0:T(8,128)S(1)}, u32[]{:S(2)}, u32[]{:S(2)}) collective-permute-start(f32[2,128,512]{1,2,0:T(8,128)S(1)} %collective-permute-done), channel_id=1, source_target_pairs={{0,504},{8,0},{16,8},{24,16},{32,24},{40,32},{48,40},{56,48},{64,5... | collective-permute-start | bytes 1572872 | tf_op jit(solution)/shard_map/ppermute | solution.py:18
  157.1 16.8 %collective-permute-start.2 = (f32[2,128,512]{1,2,0:T(8,128)S(1)}, f32[2,128,512]{1,2,0:T(8,128)S(1)}, u32[]{:S(2)}, u32[]{:S(2)}) collective-permute-start(f32[2,128,512]{1,2,0:T(8,128)S(1)} %collective-permute-done.1), channel_id=1, source_target_pairs={{0,504},{8,0},{16,8},{24,16},{32,24},{40,32},{48,40},{56,48},{64,5... | collective-permute-start | bytes 1572872 | tf_op jit(solution)/shard_map/ppermute | solution.py:18
  173.9 19.0 %collective-permute-start.3 = (f32[2,128,512]{1,2,0:T(8,128)S(1)}, f32[2,128,512]{1,2,0:T(8,128)S(1)}, u32[]{:S(2)}, u32[]{:S(2)}) collective-permute-start(f32[2,128,512]{1,2,0:T(8,128)S(1)} %collective-permute-done.2), channel_id=1, source_target_pairs={{0,504},{8,0},{16,8},{24,16},{32,24},{40,32},{48,40},{56,48},{64,5... | collective-permute-start | bytes 1572872 | tf_op jit(solution)/shard_map/ppermute | solution.py:18
  190.6 2.5 copy-start.1
  195.4 9.9 %collective-permute-start.4 = (f32[2,1,256]{2,0,1:T(2,128)S(1)}, f32[2,1,256]{2,0,1:T(2,128)S(1)}, u32[]{:S(2)}, u32[]{:S(2)}) collective-permute-start(f32[2,1,256]{2,0,1:T(2,128)S(1)} %get-tuple-element.9), channel_id=1, source_target_pairs={{0,1},{1,2},{2,3},{3,4},{4,5},{5,6},{6,7},{8,9},{9,10},{10,11},{11... | collective-permute-start | bytes 6152 | tf_op jit(solution)/shard_map/ppermute | solution.py:28
  204.0 13.0 %collective-permute-start.5 = (f32[2,1,256]{2,0,1:T(2,128)S(1)}, f32[2,1,256]{2,0,1:T(2,128)S(1)}, u32[]{:S(2)}, u32[]{:S(2)}) collective-permute-start(f32[2,1,256]{2,0,1:T(2,128)S(1)} %get-tuple-element.10), channel_id=1, source_target_pairs={{1,0},{2,1},{3,2},{4,3},{5,4},{6,5},{7,6},{9,8},{10,9},{11,10},{12... | collective-permute-start | bytes 6152 | tf_op jit(solution)/shard_map/ppermute | solution.py:29
Sparse Core Ops, SparseCore 0:
  10.6 121.9 all-gather.1
where the time goes:
time: 272 us
  waiting for transfers between devices  141 us (52%)
  blocking collectives  45 us (17%)
  starting transfers between devices  44.2 us (16%)
  between operations  13.7 us (5%)
  matrix products  13.6 us (5%)
  other arithmetic  11.6 us (4%)
    all_gather x1, waiting for transfers between devices, body(): piece = lax.all_gather(spectra, 'strip', axis=1, tiled=True)  116 us
    all_to_all x1, blocking collectives, body(): lax.all_to_all(filtered, 'sub', split_axis=2, concat_axis=0, tiled=True)  45 us
    ppermute x4, starting transfers between devices, from_behind(): return lax.ppermute(value, axis, pairs)  34.3 us
    ppermute x4, waiting for transfers between devices, from_behind(): return lax.ppermute(value, axis, pairs)  13.5 us
    ppermute x1, waiting for transfers between devices, extended(): after = lax.ppermute(leading, axis, down)  11.7 us
    another operation x4, other arithmetic  9.06 us
    ppermute x1, starting transfers between devices, extended(): before = lax.ppermute(last, axis, up)  8.55 us
    dot_general x4, matrix products, body(): jnp.einsum('ab,bmn->amn', jnp.asarray(window_mask(block_offset, sub_dev))...  8.05 us
  transfers between devices with their start and end apart: 7, of which 4 were waited for; matrix products, arithmetic and copies ran while one was open for 7% of the time, Pallas kernels for 0%

commit v1 on v0

--- a/solution.py
+++ b/solution.py
@@ -102,7 +102,9 @@
     columns = column_table(spectra.shape[2] // 2, COLS)
     table = row_table(own_rows, KR, ROWS)
     passes = (WIN - 2 + sub_dev) // sub_dev
-    piece = lax.all_gather(spectra, "strip", axis=1, tiled=True)
+    piece = jnp.concatenate(
+        lax.all_to_all(jnp.stack([spectra] * lax.axis_size("strip")), "strip", 0, 0), axis=1
+    )
     sample_index = jnp.arange(piece.shape[1], dtype=jnp.int32)
     shifted = apply_phase(
         jnp.einsum("skc,cn->skn", piece, columns, preferred_element_type=jnp.float32),

time: 272 us -> 235 us (0.86)
  waiting for transfers between devices: 141 us -> 49.5 us
  starting transfers between devices: 44.2 us -> 110 us
  between operations: 13.7 us -> 0.31 us
  local copies, waits for them, and re-layouts: 2.56 us -> 6.14 us
    all_gather x1 -> x0, waiting for transfers between devices: 116 us -> none  [body(): piece = lax.all_gather(spectra, 'strip', axis=1, tiled=True)]
    ppermute x4, starting transfers between devices: 34.3 us -> 78.1 us  [from_behind(): return lax.ppermute(value, axis, pairs)]
    all_to_all x0 -> x1, waiting for transfers between devices: none -> 39.2 us  [body(): lax.all_to_all(jnp.stack([spectra] * lax.axis_size('strip')), 'strip', 0, 0)]
    all_to_all x0 -> x1, starting transfers between devices: none -> 18.2 us  [body(): lax.all_to_all(jnp.stack([spectra] * lax.axis_size('strip')), 'strip', 0, 0)]
    ppermute x1, waiting for transfers between devices: 11.7 us -> 0.01 us  [extended(): after = lax.ppermute(leading, axis, down)]
    ppermute x1, starting transfers between devices: 8.55 us -> 12.7 us  [extended(): before = lax.ppermute(last, axis, up)]
    ppermute x4, waiting for transfers between devices: 13.5 us -> 9.55 us  [from_behind(): return lax.ppermute(value, axis, pairs)]
  transfers between devices with their start and end apart: 7 -> 7, of which waited for: 4 -> 4; matrix products, arithmetic and copies ran while one was open for 7% -> 8% of each run, Pallas kernels for 0% -> 0%
where the time goes in v1:
time: 235 us
  starting transfers between devices  110 us (47%)
  waiting for transfers between devices  49.5 us (21%)
  blocking collectives  45 us (19%)
  other arithmetic  11.8 us (5%)
  matrix products  11.8 us (5%)
  local copies, waits for them, and re-layouts  6.14 us (3%)
    ppermute x4, starting transfers between devices, from_behind(): return lax.ppermute(value, axis, pairs)  78.1 us
    all_to_all x1, blocking collectives, body(): lax.all_to_all(filtered, 'sub', split_axis=2, concat_axis=0, tiled=True)  45 us
    all_to_all x1, waiting for transfers between devices, body(): lax.all_to_all(jnp.stack([spectra] * lax.axis_size('strip')), 'strip', 0, 0)  39.2 us
    all_to_all x1, starting transfers between devices, body(): lax.all_to_all(jnp.stack([spectra] * lax.axis_size('strip')), 'strip', 0, 0)  18.2 us
    ppermute x1, starting transfers between devices, extended(): before = lax.ppermute(last, axis, up)  12.7 us
    another operation x4, other arithmetic  9.91 us
    ppermute x4, waiting for transfers between devices, from_behind(): return lax.ppermute(value, axis, pairs)  9.55 us
    dot_general x4, matrix products, body(): jnp.einsum('ab,bmn->amn', jnp.asarray(window_mask(block_offset, sub_dev))...  7.93 us
  transfers between devices with their start and end apart: 7, of which 4 were waited for; matrix products, arithmetic and copies ran while one was open for 8% of the time, Pallas kernels for 0%

profile of v1, /device:TPU:1, one launch (start us, length us, event | category | flops | bytes accessed | tf_op | source)
XLA Modules:
  0.0 235.0 jit_solution(6658816487928637441)
XLA Ops:
  0.0 2.5 %stack.2 = bf16[8,2,32,2048]{3,2,1,0:T(8,128)(2,1)} broadcast(bf16[2,32,2048]{2,1,0:T(8,128)(2,1)} %param.7), dimensions={1,2,3} | broadcast | bytes 2359296 | tf_op jit(solution)/shard_map/stack | solution.py:106
  2.5 18.2 %all-to-all-start = ((bf16[8,2,32,2048]{3,2,1,0:T(8,128)(2,1)}), bf16[8,2,32,2048]{3,2,1,0:T(8,128)(2,1)S(1)}, u32[]{:S(2)}, u32[]{:S(2)}) async-start(bf16[8,2,32,2048]{3,2,1,0:T(8,128)(2,1)} %stack.2), calls=%async_computation | async-start | bytes 4194304 | tf_op jit(solution)/shard_map/all_to_all | solution.py:106
  20.8 4.0 %fusion.15 = bf16[1024,256]{0,1:T(8,128)(2,1)S(1)} fusion(), kind=kLoop, calls=%fused_computation.27 | loop fusion | flops 4456448 | bytes 524288 | tf_op jit(solution)/shard_map/convert.9
  24.8 5.2 %negate_convert_fusion = (bf16[1024,256]{0,1:T(8,128)(2,1)S(1)}, bf16[1024,256]{0,1:T(8,128)(2,1)}) fusion(), kind=kLoop, calls=%fused_computation.21 | loop fusion | flops 5242880 | bytes 1048576 | tf_op jit(solution)/shard_map/convert.6
  30.0 0.0 copy-done.2
  30.0 0.1 fusion.55
  30.1 0.6 multiply_convert_fusion.2
  30.7 39.2 %all-to-all-done = bf16[8,2,32,2048]{3,2,1,0:T(8,128)(2,1)S(1)} async-done(((bf16[8,2,32,2048]{3,2,1,0:T(8,128)(2,1)}), bf16[8,2,32,2048]{3,2,1,0:T(8,128)(2,1)S(1)}, u32[]{:S(2)}, u32[]{:S(2)}) %all-to-all-start) | async-done | bytes 2097184 | tf_op jit(solution)/shard_map/all_to_all | solution.py:106
  70.0 0.2 copy.35
  70.2 0.8 copy-done
  71.0 1.3 fusion.7
  72.3 0.1 subtract_convert_fusion
  72.4 0.3 convolution_bitcast_fusion
  72.8 0.0 copy-start.1
  72.8 0.1 slice_subtract_fusion
  72.9 3.8 %collective-permute-start = (f32[2,128,512]{1,2,0:T(8,128)S(1)}, f32[2,128,512]{1,2,0:T(8,128)S(1)}, u32[]{:S(2)}, u32[]{:S(2)}) collective-permute-start(f32[2,128,512]{1,2,0:T(8,128)S(1)} %pad_maximum_fusion), channel_id=1, source_target_pairs={{0,504},{8,0},{16,8},{24,16},{32,24},{40,32},{48,40},{56,48},{64,5... | collective-permute-start | bytes 1572872 | tf_op jit(solution)/shard_map/ppermute | solution.py:18
  76.7 8.0 %collective-permute-done = f32[2,128,512]{1,2,0:T(8,128)S(1)} collective-permute-done((f32[2,128,512]{1,2,0:T(8,128)S(1)}, f32[2,128,512]{1,2,0:T(8,128)S(1)}, u32[]{:S(2)}, u32[]{:S(2)}) %collective-permute-start) | collective-permute-done | bytes 524320 | tf_op jit(solution)/shard_map/ppermute | solution.py:18
  84.7 41.0 %collective-permute-start.1 = (f32[2,128,512]{1,2,0:T(8,128)S(1)}, f32[2,128,512]{1,2,0:T(8,128)S(1)}, u32[]{:S(2)}, u32[]{:S(2)}) collective-permute-start(f32[2,128,512]{1,2,0:T(8,128)S(1)} %collective-permute-done), channel_id=1, source_target_pairs={{0,504},{8,0},{16,8},{24,16},{32,24},{40,32},{48,40},{56,48},{64,5... | collective-permute-start | bytes 1572872 | tf_op jit(solution)/shard_map/ppermute | solution.py:18
  125.7 1.5 collective-permute-done.1
  127.2 18.6 %collective-permute-start.2 = (f32[2,128,512]{1,2,0:T(8,128)S(1)}, f32[2,128,512]{1,2,0:T(8,128)S(1)}, u32[]{:S(2)}, u32[]{:S(2)}) collective-permute-start(f32[2,128,512]{1,2,0:T(8,128)S(1)} %collective-permute-done.1), channel_id=1, source_target_pairs={{0,504},{8,0},{16,8},{24,16},{32,24},{40,32},{48,40},{56,48},{64,5... | collective-permute-start | bytes 1572872 | tf_op jit(solution)/shard_map/ppermute | solution.py:18
  145.8 0.2 copy.36
  146.1 0.0 copy-done.1
  146.1 1.9 fusion.72
  148.0 0.2 copy.37
  148.2 1.9 convolution_add_fusion.3
  150.2 0.2 copy.38
  150.4 0.0 collective-permute-done.2
  150.4 14.8 %collective-permute-start.3 = (f32[2,128,512]{1,2,0:T(8,128)S(1)}, f32[2,128,512]{1,2,0:T(8,128)S(1)}, u32[]{:S(2)}, u32[]{:S(2)}) collective-permute-start(f32[2,128,512]{1,2,0:T(8,128)S(1)} %collective-permute-done.2), channel_id=1, source_target_pairs={{0,504},{8,0},{16,8},{24,16},{32,24},{40,32},{48,40},{56,48},{64,5... | collective-permute-start | bytes 1572872 | tf_op jit(solution)/shard_map/ppermute | solution.py:18
  165.2 1.9 convolution_add_fusion.2
  167.2 0.0 copy-start.3
  167.2 0.2 copy.39
  167.4 2.0 convolution_add_fusion.1
  169.4 0.0 collective-permute-done.3
  169.4 0.2 copy.40
  169.7 2.0 fusion.8
  171.7 0.2 fusion.24
  172.0 1.3 collective-permute-start.5
  173.3 12.7 %collective-permute-start.4 = (f32[2,1,256]{2,0,1:T(2,128)S(1)}, f32[2,1,256]{2,0,1:T(2,128)S(1)}, u32[]{:S(2)}, u32[]{:S(2)}) collective-permute-start(f32[2,1,256]{2,0,1:T(2,128)S(1)} %get-tuple-element.9), channel_id=1, source_target_pairs={{0,1},{1,2},{2,3},{3,4},{4,5},{5,6},{6,7},{8,9},{9,10},{10,11},{11... | collective-permute-start | bytes 6152 | tf_op jit(solution)/shard_map/ppermute | solution.py:28
  186.0 0.0 collective-permute-done.5
  186.0 0.7 collective-permute-done.4
  186.7 0.5 select_maximum_fusion
  187.2 1.0 fusion.19
  188.1 0.2 copy.41
  188.3 45.0 %all_to_all.23 = f32[2,128,256]{1,0,2:T(2,128)S(1)} all-to-all(f32[2,128,256]{1,0,2:T(2,128)S(1)} %copy.41), channel_id=1, replica_groups=mesh['sub'=64,'strip'=8] {'sub'}, dimensions={2} | all-to-all | bytes 524288 | tf_op jit(solution)/shard_map/all_to_all | solution.py:139
  233.3 0.2 copy.43
  233.5 0.1 copy.44
  233.7 0.4 fusion.26
  234.1 0.9 copy.45
  (8 shorter events, 0.1 us)
Async XLA Ops:
  2.5 27.4 %copy-start.2 = (s32[2]{0:T(128)S(1)}, s32[2]{0:T(128)}, u32[]{:S(2)}) copy-start(s32[2]{0:T(128)} %param.8) | copy-start | bytes 28
  2.5 67.4 %all-to-all-start = ((bf16[8,2,32,2048]{3,2,1,0:T(8,128)(2,1)}), bf16[8,2,32,2048]{3,2,1,0:T(8,128)(2,1)S(1)}, u32[]{:S(2)}, u32[]{:S(2)}) async-start(bf16[8,2,32,2048]{3,2,1,0:T(8,128)(2,1)} %stack.2), calls=%async_computation | async-start | bytes 4194304 | tf_op jit(solution)/shard_map/all_to_all | solution.py:106
  70.0 1.0 copy-start
  72.8 73.3 %copy-start.1 = (f32[2,2,1]{1,0,2:T(2,128)S(1)}, f32[2,2,1]{1,0,2:T(2,128)}, u32[]{:S(2)}) copy-start(f32[2,2,1]{1,0,2:T(2,128)} %constant.88) | copy-start | bytes 52
  72.9 11.8 %collective-permute-start = (f32[2,128,512]{1,2,0:T(8,128)S(1)}, f32[2,128,512]{1,2,0:T(8,128)S(1)}, u32[]{:S(2)}, u32[]{:S(2)}) collective-permute-start(f32[2,128,512]{1,2,0:T(8,128)S(1)} %pad_maximum_fusion), channel_id=1, source_target_pairs={{0,504},{8,0},{16,8},{24,16},{32,24},{40,32},{48,40},{56,48},{64,5... | collective-permute-start | bytes 1572872 | tf_op jit(solution)/shard_map/ppermute | solution.py:18
  84.7 42.5 %collective-permute-start.1 = (f32[2,128,512]{1,2,0:T(8,128)S(1)}, f32[2,128,512]{1,2,0:T(8,128)S(1)}, u32[]{:S(2)}, u32[]{:S(2)}) collective-permute-start(f32[2,128,512]{1,2,0:T(8,128)S(1)} %collective-permute-done), channel_id=1, source_target_pairs={{0,504},{8,0},{16,8},{24,16},{32,24},{40,32},{48,40},{56,48},{64,5... | collective-permute-start | bytes 1572872 | tf_op jit(solution)/shard_map/ppermute | solution.py:18
  127.2 23.2 %collective-permute-start.2 = (f32[2,128,512]{1,2,0:T(8,128)S(1)}, f32[2,128,512]{1,2,0:T(8,128)S(1)}, u32[]{:S(2)}, u32[]{:S(2)}) collective-permute-start(f32[2,128,512]{1,2,0:T(8,128)S(1)} %collective-permute-done.1), channel_id=1, source_target_pairs={{0,504},{8,0},{16,8},{24,16},{32,24},{40,32},{48,40},{56,48},{64,5... | collective-permute-start | bytes 1572872 | tf_op jit(solution)/shard_map/ppermute | solution.py:18
  150.4 19.0 %collective-permute-start.3 = (f32[2,128,512]{1,2,0:T(8,128)S(1)}, f32[2,128,512]{1,2,0:T(8,128)S(1)}, u32[]{:S(2)}, u32[]{:S(2)}) collective-permute-start(f32[2,128,512]{1,2,0:T(8,128)S(1)} %collective-permute-done.2), channel_id=1, source_target_pairs={{0,504},{8,0},{16,8},{24,16},{32,24},{40,32},{48,40},{56,48},{64,5... | collective-permute-start | bytes 1572872 | tf_op jit(solution)/shard_map/ppermute | solution.py:18
  167.2 2.5 %copy-start.3 = (f32[2,2,1]{1,0,2:T(2,128)S(1)}, f32[2,2,1]{1,0,2:T(2,128)}, u32[]{:S(2)}) copy-start(f32[2,2,1]{1,0,2:T(2,128)} %constant.89) | copy-start | bytes 52
  172.0 14.0 %collective-permute-start.5 = (f32[2,1,256]{2,0,1:T(2,128)S(1)}, f32[2,1,256]{2,0,1:T(2,128)S(1)}, u32[]{:S(2)}, u32[]{:S(2)}) collective-permute-start(f32[2,1,256]{2,0,1:T(2,128)S(1)} %get-tuple-element.10), channel_id=1, source_target_pairs={{1,0},{2,1},{3,2},{4,3},{5,4},{6,5},{7,6},{9,8},{10,9},{11,10},{12... | collective-permute-start | bytes 6152 | tf_op jit(solution)/shard_map/ppermute | solution.py:29
  173.3 13.4 %collective-permute-start.4 = (f32[2,1,256]{2,0,1:T(2,128)S(1)}, f32[2,1,256]{2,0,1:T(2,128)S(1)}, u32[]{:S(2)}, u32[]{:S(2)}) collective-permute-start(f32[2,1,256]{2,0,1:T(2,128)S(1)} %get-tuple-element.9), channel_id=1, source_target_pairs={{0,1},{1,2},{2,3},{3,4},{4,5},{5,6},{6,7},{8,9},{9,10},{10,11},{11... | collective-permute-start | bytes 6152 | tf_op jit(solution)/shard_map/ppermute | solution.py:28
